TPU v7x, 32 devices: a whole 2x2x4 slice. The times are simulated.
32 devices in a mesh: dp: 2 (over x), fsdp: 16 (over z, y, core).
Axes of the slice: x: 2, y: 2, z: 4, core: 2. Of those that a mesh axis runs over, the one named last changes fastest.
Arguments:
- inputs: bfloat16 [16384, 1024], P(('dp', 'fsdp')), may hold values from -6 to 6
- doc_lengths: int32 [32, 4], P(('dp', 'fsdp')), may hold values from 1 to 256, 512 in all within a row
- w_aq: bfloat16 [1024, 96], P(('dp', 'fsdp')), may hold values from -0.3125 to 0.3125
- w_bq: bfloat16 [1024, 384], P(('dp', 'fsdp')), may hold values from -0.3125 to 0.3125
- w_ak: bfloat16 [1024, 32], P(('dp', 'fsdp')), may hold values from -0.3125 to 0.3125
- w_bk: bfloat16 [1024, 128], P(('dp', 'fsdp')), may hold values from -0.3125 to 0.3125
- w_av: bfloat16 [1024, 32], P(('dp', 'fsdp')), may hold values from -0.1875 to 0.1875
- w_bv: bfloat16 [1024, 128], P(('dp', 'fsdp')), may hold values from -0.1875 to 0.1875
- w_out: bfloat16 [1024, 1024], P(('dp', 'fsdp')), may hold values from -1.5 to 1.5
- w_gate: bfloat16 [1024, 2816], P(('dp', 'fsdp')), may hold values from -0.1875 to 0.1875
- w_up: bfloat16 [1024, 2816], P(('dp', 'fsdp')), may hold values from -0.1875 to 0.1875
- w_down: bfloat16 [2816, 1024], P(('dp', 'fsdp')), may hold values from -0.109375 to 0.109375
- gain_attn: bfloat16 [1024], P(('dp', 'fsdp')), may hold values from 0.5 to 1.5
- gain_ffn: bfloat16 [1024], P(('dp', 'fsdp')), may hold values from 0.5 to 1.5
- cotangent: bfloat16 [16384, 1024], P(('dp', 'fsdp')), may hold values from -6 to 6
Outputs:
- outputs: bfloat16 [16384, 1024], P(('dp', 'fsdp'))
- input_grad: float32 [16384, 1024], P(('dp', 'fsdp'))
- grad_aq: float32 [1024, 96], P(('dp', 'fsdp'))
- grad_bq: float32 [1024, 384], P(('dp', 'fsdp'))
- grad_ak: float32 [1024, 32], P(('dp', 'fsdp'))
- grad_bk: float32 [1024, 128], P(('dp', 'fsdp'))
- grad_av: float32 [1024, 32], P(('dp', 'fsdp'))
- grad_bv: float32 [1024, 128], P(('dp', 'fsdp'))
- grad_out: float32 [1024, 1024], P(('dp', 'fsdp'))
- grad_gate: float32 [1024, 2816], P(('dp', 'fsdp'))
- grad_up: float32 [1024, 2816], P(('dp', 'fsdp'))
- grad_down: float32 [2816, 1024], P(('dp', 'fsdp'))
- grad_gain_attn: float32 [1024], P(('dp', 'fsdp'))
- grad_gain_ffn: float32 [1024], P(('dp', 'fsdp'))
Inputs may be any that keep to these rules, and one draw needn't show every extreme that they name: `doc_lengths`: each row's 4 document lengths sum to 512.
All inputs are finite; a program needn't handle non-finite values.
Results may differ from a plain program's by a relative error of at most 0.013.
The roundings to bfloat16 on the way count: a program that leaves them out, or rounds other values in their place, can miss the bound.
Values may be sent and summed in bfloat16 or wider, within the bound.
A program may use at most 256 MiB of HBM per device.

v0:
```python
import math

import jax
import jax.numpy as jnp
from jax import lax
from jax.sharding import PartitionSpec as P

HEADS = 16
HEAD_DIM = 64
RANK_Q = 6
RANK_KV = 2
FF = 2816


EPSILON = 1e-06
PRECISE = lax.Precision.HIGHEST


def factor_columns():
    return [
        RANK_Q * HEADS,
        RANK_Q * HEAD_DIM,
        RANK_KV * HEADS,
        RANK_KV * HEAD_DIM,
        RANK_KV * HEADS,
        RANK_KV * HEAD_DIM,
    ]


def split_columns(matrix):
    pieces = []
    offset = 0
    for columns in factor_columns():
        pieces.append(matrix[:, offset : offset + columns])
        offset += columns
    return pieces


def doc_layout(lengths, length):
    doc_ends = jnp.cumsum(lengths)
    doc_starts = doc_ends - lengths
    places = jnp.arange(length, dtype=jnp.int32)
    segment = jnp.sum((places[:, None] >= doc_ends[None, :]).astype(jnp.int32), axis=1)
    owner = segment[:, None] == jnp.arange(lengths.shape[0], dtype=jnp.int32)[None, :]
    doc_first = jnp.sum(jnp.where(owner, doc_starts[None, :], 0), axis=1)
    return (segment, (places - doc_first).astype(jnp.float32))


def rotation(places):
    halfway = HEAD_DIM // 2
    freqs = jnp.exp(-math.log(10000.0) * jnp.arange(halfway, dtype=jnp.float32) / halfway)
    angles = places[..., None] * freqs
    return (jnp.cos(angles), jnp.sin(angles))


def rotate(factor, cos_table, sin_table):
    halfway = factor.shape[-1] // 2
    front_part = factor[..., :halfway]
    back_part = factor[..., halfway:]
    cos_part = cos_table[..., None, :]
    sin_part = sin_table[..., None, :]
    return jnp.concatenate(
        [
            front_part * cos_part - back_part * sin_part,
            front_part * sin_part + back_part * cos_part,
        ],
        axis=-1,
    )


def normalize(values, gain):
    scaling = lax.rsqrt(jnp.mean(values * values, axis=-1, keepdims=True) + EPSILON)
    unit_vals = values * scaling
    return (unit_vals * gain, unit_vals, scaling)


def norm_back(incoming, unit_vals, scaling, gain):
    unit_grad = incoming * gain
    grad_in = scaling * (
        unit_grad - unit_vals * jnp.mean(unit_grad * unit_vals, axis=-1, keepdims=True)
    )
    return (grad_in, jnp.sum(incoming * unit_vals, axis=0))


def block_scores(query_part, keys_low, seg_part, segment, place_part, places):
    scaling = HEAD_DIM ** (-0.5)
    scores = (
        jnp.einsum("thd,shd->hts", query_part, keys_low, preferred_element_type=jnp.float32)
        * scaling
    )
    allowed = (seg_part[:, None] == segment[None, :]) & (places[None, :] <= place_part[:, None])
    return jnp.where(allowed[None], scores, -1e30)


def attend_forward(queries, keys_low, values, segment):
    length = queries.shape[0]
    block_rows = min(512, length)
    places = jnp.arange(length, dtype=jnp.int32)

    def one_block(block_index):
        masked = block_scores(queries, keys_low, segment, segment, places, places)
        row_peak = jnp.max(masked, axis=-1, keepdims=True)
        exp_terms = jnp.exp(masked - row_peak)
        row_total = jnp.sum(exp_terms, axis=-1, keepdims=True)
        attn_probs = (exp_terms / row_total).astype(jnp.bfloat16)
        attended = jnp.einsum(
            "hts,shd->thd", attn_probs, values, preferred_element_type=jnp.float32
        )
        return (attended, (row_peak + jnp.log(row_total))[..., 0])

    attended, log_totals = lax.map(one_block, jnp.arange(length // block_rows, dtype=jnp.int32))
    return (attended.reshape(length, HEADS, HEAD_DIM), log_totals)


def attend_backward(queries, keys_low, values, segment, log_totals, mixed_grad):
    length = queries.shape[0]
    block_rows = min(512, length)
    places = jnp.arange(length, dtype=jnp.int32)
    scaling = HEAD_DIM ** (-0.5)

    def one_block(running, block_index):
        key_grad, value_grad = running
        masked = block_scores(queries, keys_low, segment, segment, places, places)
        attn_probs = jnp.exp(masked - log_totals[block_index][..., None])
        probs_low = attn_probs.astype(jnp.bfloat16)
        value_grad = value_grad + jnp.einsum(
            "hts,thd->shd", probs_low, mixed_grad, preferred_element_type=jnp.float32
        )
        probs_grad = jnp.einsum(
            "thd,shd->hts", mixed_grad, values, preferred_element_type=jnp.float32
        )
        inner_sum = jnp.sum(attn_probs * probs_grad, axis=-1, keepdims=True)
        score_grad = (attn_probs * (probs_grad - inner_sum)).astype(jnp.bfloat16)
        query_grad = (
            jnp.einsum("hts,shd->thd", score_grad, keys_low, preferred_element_type=jnp.float32)
            * scaling
        )
        key_grad = (
            key_grad
            + jnp.einsum("hts,thd->shd", score_grad, queries, preferred_element_type=jnp.float32)
            * scaling
        )
        return ((key_grad, value_grad), query_grad)

    empty = jnp.zeros((length, HEADS, HEAD_DIM), jnp.float32)
    (key_grad, value_grad), query_grad = lax.scan(
        one_block, (empty, empty), jnp.arange(length // block_rows, dtype=jnp.int32)
    )
    return (query_grad.reshape(length, HEADS, HEAD_DIM), key_grad, value_grad)


def factor_back(full_grad, a_part, b_part, rank_count):
    a_grad = jnp.einsum("thd,trd->trh", full_grad, b_part, precision=PRECISE) / rank_count
    b_grad = jnp.einsum("thd,trh->trd", full_grad, a_part, precision=PRECISE) / rank_count
    return (a_grad, b_grad)


def local(
    inputs,
    doc_lengths,
    w_aq,
    w_bq,
    w_ak,
    w_bk,
    w_av,
    w_bv,
    w_out,
    w_gate,
    w_up,
    w_down,
    gain_attn,
    gain_ffn,
    cotangent,
):
    length = inputs.shape[0]
    joined_local = jnp.concatenate([w_aq, w_bq, w_ak, w_bk, w_av, w_bv], axis=1)
    factor_w, out_w, gain_one = (
        lax.all_gather(joined_local, ("dp", "fsdp"), axis=0, tiled=True),
        lax.all_gather(w_out, ("dp", "fsdp"), axis=0, tiled=True),
        lax.all_gather(gain_attn, ("dp", "fsdp"), axis=0, tiled=True),
    )
    segment, places = doc_layout(doc_lengths[0], length)
    cos_table, sin_table = rotation(places)
    start_vals = inputs.astype(jnp.float32)
    normed_one, unit_one, scale_one = normalize(start_vals, gain_one.astype(jnp.float32))
    normed_low = normed_one.astype(jnp.bfloat16)
    factors = jnp.dot(normed_low, factor_w, preferred_element_type=jnp.float32)
    pieces = split_columns(factors)
    a_q = pieces[0].reshape(length, RANK_Q, HEADS)
    b_q = pieces[1].reshape(length, RANK_Q, HEAD_DIM)
    a_k = pieces[2].reshape(length, RANK_KV, HEADS)
    b_k = pieces[3].reshape(length, RANK_KV, HEAD_DIM)
    a_v = pieces[4].reshape(length, RANK_KV, HEADS)
    b_v = pieces[5].reshape(length, RANK_KV, HEAD_DIM)
    bq_rot = rotate(b_q, cos_table, sin_table)
    bk_rot = rotate(b_k, cos_table, sin_table)
    queries = (jnp.einsum("trh,trd->thd", a_q, bq_rot, precision=PRECISE) / RANK_Q).astype(
        jnp.bfloat16
    )
    keys_low = (jnp.einsum("trh,trd->thd", a_k, bk_rot, precision=PRECISE) / RANK_KV).astype(
        jnp.bfloat16
    )
    values = (jnp.einsum("trh,trd->thd", a_v, b_v, precision=PRECISE) / RANK_KV).astype(
        jnp.bfloat16
    )
    attended, log_totals = attend_forward(queries, keys_low, values, segment)
    mixed = attended.astype(jnp.bfloat16).reshape(length, HEADS * HEAD_DIM)
    resid = start_vals + jnp.dot(mixed, out_w, preferred_element_type=jnp.float32)
    gate_w, up_w, down_w, gain_two = (
        lax.all_gather(w_gate, ("dp", "fsdp"), axis=0, tiled=True),
        lax.all_gather(w_up, ("dp", "fsdp"), axis=0, tiled=True),
        lax.all_gather(w_down, ("dp", "fsdp"), axis=0, tiled=True),
        lax.all_gather(gain_ffn, ("dp", "fsdp"), axis=0, tiled=True),
    )
    normed_two, unit_two, scale_two = normalize(resid, gain_two.astype(jnp.float32))
    normed_two_low = normed_two.astype(jnp.bfloat16)
    gate_act = jnp.dot(normed_two_low, gate_w, preferred_element_type=jnp.float32)
    up_act = jnp.dot(normed_two_low, up_w, preferred_element_type=jnp.float32)
    hidden = (jax.nn.silu(gate_act) * up_act).astype(jnp.bfloat16)
    result = resid + jnp.dot(hidden, down_w, preferred_element_type=jnp.float32)
    outputs = result.astype(jnp.bfloat16)
    gate_w, up_w, down_w, gain_two = (
        lax.all_gather(w_gate, ("dp", "fsdp"), axis=0, tiled=True),
        lax.all_gather(w_up, ("dp", "fsdp"), axis=0, tiled=True),
        lax.all_gather(w_down, ("dp", "fsdp"), axis=0, tiled=True),
        lax.all_gather(gain_ffn, ("dp", "fsdp"), axis=0, tiled=True),
    )
    hidden_grad = jnp.einsum("tc,fc->tf", cotangent, down_w, preferred_element_type=jnp.float32)
    down_wgrad = jnp.einsum("tf,tc->fc", hidden, cotangent, preferred_element_type=jnp.float32)
    sig_vals = jax.nn.sigmoid(gate_act)
    gate_grad = (hidden_grad * up_act * sig_vals * (1.0 + gate_act * (1.0 - sig_vals))).astype(
        jnp.bfloat16
    )
    up_grad = (hidden_grad * jax.nn.silu(gate_act)).astype(jnp.bfloat16)
    normed_two_grad = jnp.einsum("tf,cf->tc", gate_grad, gate_w, preferred_element_type=jnp.float32)
    normed_two_grad = normed_two_grad + jnp.einsum(
        "tf,cf->tc", up_grad, up_w, preferred_element_type=jnp.float32
    )
    resid_norm_grad, gain_two_grad = norm_back(
        normed_two_grad, unit_two, scale_two, gain_two.astype(jnp.float32)
    )
    resid_grad = cotangent.astype(jnp.float32) + resid_norm_grad
    gate_rows = jnp.einsum(
        "tc,tf->cf", normed_two_low, gate_grad, preferred_element_type=jnp.float32
    )
    up_rows = jnp.einsum("tc,tf->cf", normed_two_low, up_grad, preferred_element_type=jnp.float32)
    gate_up_shard = lax.psum_scatter(
        jnp.concatenate([gate_rows, up_rows], axis=1),
        ("dp", "fsdp"),
        scatter_dimension=0,
        tiled=True,
    )
    gate_shard = gate_up_shard[:, :FF]
    up_shard = gate_up_shard[:, FF:]
    down_shard, gain_two_shard = (
        lax.psum_scatter(down_wgrad, ("dp", "fsdp"), scatter_dimension=0, tiled=True),
        lax.psum_scatter(gain_two_grad, ("dp", "fsdp"), scatter_dimension=0, tiled=True),
    )
    factor_w, out_w, gain_one = (
        lax.all_gather(joined_local, ("dp", "fsdp"), axis=0, tiled=True),
        lax.all_gather(w_out, ("dp", "fsdp"), axis=0, tiled=True),
        lax.all_gather(gain_attn, ("dp", "fsdp"), axis=0, tiled=True),
    )
    branch_grad = resid_grad.astype(jnp.bfloat16)
    out_wgrad = jnp.einsum("tc,td->cd", mixed, branch_grad, preferred_element_type=jnp.float32)
    mixed_grad = jnp.einsum("td,cd->tc", branch_grad, out_w, preferred_element_type=jnp.float32)
    mixed_grad = mixed_grad.astype(jnp.bfloat16).reshape(length, HEADS, HEAD_DIM)
    query_grad, key_grad, value_grad = attend_backward(
        queries, keys_low, values, segment, log_totals, mixed_grad
    )
    a_q_grad, bq_rot_grad = factor_back(query_grad, a_q, bq_rot, RANK_Q)
    a_k_grad, bk_rot_grad = factor_back(key_grad, a_k, bk_rot, RANK_KV)
    a_v_grad, b_v_grad = factor_back(value_grad, a_v, b_v, RANK_KV)
    neg_sin = -sin_table
    b_q_grad = rotate(bq_rot_grad, cos_table, neg_sin)
    b_k_grad = rotate(bk_rot_grad, cos_table, neg_sin)
    factor_grad = jnp.concatenate(
        [
            part.reshape(length, -1)
            for part in (a_q_grad, b_q_grad, a_k_grad, b_k_grad, a_v_grad, b_v_grad)
        ],
        axis=1,
    ).astype(jnp.bfloat16)
    factor_wgrad = jnp.einsum(
        "td,tc->dc", normed_low, factor_grad, preferred_element_type=jnp.float32
    )
    normed_one_grad = jnp.einsum(
        "tc,dc->td", factor_grad, factor_w, preferred_element_type=jnp.float32
    )
    input_norm_grad, gain_one_grad = norm_back(
        normed_one_grad, unit_one, scale_one, gain_one.astype(jnp.float32)
    )
    input_grad = resid_grad + input_norm_grad
    factor_shard, out_shard, gain_one_shard = (
        lax.psum_scatter(factor_wgrad, ("dp", "fsdp"), scatter_dimension=0, tiled=True),
        lax.psum_scatter(out_wgrad, ("dp", "fsdp"), scatter_dimension=0, tiled=True),
        lax.psum_scatter(gain_one_grad, ("dp", "fsdp"), scatter_dimension=0, tiled=True),
    )
    shard_pieces = split_columns(factor_shard)
    return (
        outputs,
        input_grad,
        shard_pieces[0],
        shard_pieces[1],
        shard_pieces[2],
        shard_pieces[3],
        shard_pieces[4],
        shard_pieces[5],
        out_shard,
        gate_shard,
        up_shard,
        down_shard,
        gain_one_shard,
        gain_two_shard,
    )


def solution(mesh):
    return jax.shard_map(
        local,
        mesh=mesh,
        in_specs=(
            P(("dp", "fsdp"), None),
            P(("dp", "fsdp"), None),
            P(("dp", "fsdp"), None),
            P(("dp", "fsdp"), None),
            P(("dp", "fsdp"), None),
            P(("dp", "fsdp"), None),
            P(("dp", "fsdp"), None),
            P(("dp", "fsdp"), None),
            P(("dp", "fsdp"), None),
            P(("dp", "fsdp"), None),
            P(("dp", "fsdp"), None),
            P(("dp", "fsdp"), None),
            P(("dp", "fsdp")),
            P(("dp", "fsdp")),
            P(("dp", "fsdp"), None),
        ),
        out_specs=(
            P(("dp", "fsdp"), None),
            P(("dp", "fsdp"), None),
            P(("dp", "fsdp"), None),
            P(("dp", "fsdp"), None),
            P(("dp", "fsdp"), None),
            P(("dp", "fsdp"), None),
            P(("dp", "fsdp"), None),
            P(("dp", "fsdp"), None),
            P(("dp", "fsdp"), None),
            P(("dp", "fsdp"), None),
            P(("dp", "fsdp"), None),
            P(("dp", "fsdp"), None),
            P(("dp", "fsdp")),
            P(("dp", "fsdp")),
        ),
        check_vma=False,
    )
```

profile of v0, /device:TPU:0, one launch (start us, length us, event | category | flops | bytes accessed | tf_op | source)
XLA Modules:
  0.0 1177.5 jit_solution(7806577278496393754)
XLA Ops:
  14.2 42.1 %all-reduce.5 = (bf16[1024]{0:T(1024)(128)(2,1)S(1)}, bf16[1024]{0:T(1024)(128)(2,1)S(1)}) all-reduce(bf16[1024]{0:T(1024)(128)(2,1)S(1)} %dynamic-update-slice, bf16[1024]{0:T(1024)(128)(2,1)S(1)} %dynamic-update-slice.1), channel_id=1, replica_groups=mesh['dp'=2,'fsdp'=16] {'dp','fsdp'}, use_global_device_ids=true, to_apply=%add | all-reduce | flops 2048 | bytes 8192
  61.2 8.9 all-gather.6.cloned.1.call-done
  81.3 9.0 fusion.45
  108.8 9.2 fusion.25
  124.8 9.3 fusion.54
  137.9 9.4 fusion.53
  147.4 8.3 fusion
  155.7 10.3 fusion.21
  170.8 26.7 %all-gather.10.cloned.1.call-done = bf16[1024,2816]{1,0:T(8,128)(2,1)} async-done(((bf16[32,2816]{1,0:T(8,128)(2,1)}), bf16[1024,2816]{1,0:T(8,128)(2,1)}) %all-gather.10.cloned.1.call-update) | async-done | bytes 5767184 | tf_op jit(solution)/shard_map/all_gather | solution.py:210
  204.9 61.5 %all-gather.12.cloned.1.call-done = bf16[1024,2816]{1,0:T(8,128)(2,1)} async-done(((bf16[32,2816]{1,0:T(8,128)(2,1)}), bf16[1024,2816]{1,0:T(8,128)(2,1)}) %all-gather.12.cloned.1.call-update) | async-done | bytes 5767184 | tf_op jit(solution)/shard_map/all_gather | solution.py:211
  274.0 61.4 %all-gather.14.cloned.1.call-done = bf16[2816,1024]{1,0:T(8,128)(2,1)} async-done(((bf16[88,1024]{1,0:T(8,128)(2,1)}), bf16[2816,1024]{1,0:T(8,128)(2,1)}) %all-gather.14.cloned.1.call-update) | async-done | bytes 5767184 | tf_op jit(solution)/shard_map/all_gather | solution.py:212
  335.5 11.3 multiply_convert_fusion.1
  363.5 9.8 fusion.18
  392.7 10.8 multiply_reduce_fusion
  403.5 12.3 %multiply_convert_fusion = bf16[16,512,512]{1,2,0:T(8,128)(2,1)S(1)} fusion(f32[16,512,512]{1,2,0:T(8,128)} %get-tuple-element.113, f32[16,512,512]{1,2,0:T(8,128)} %get-tuple-element.108, f32[16,512]{1,0:T(8,128)S(1)} %get-tuple-element.112, f32[16,512]{1,0:T(8,128)S(1)} %log_add_fusion), kind=kLoop, calls=%fused_computation.1 | loop fusion | flops 16777216 | bytes 42008576 | tf_op jit(solution)/shard_map/while/body/eval_jaxpr/convert_element_type | solution.py:133
  433.6 10.2 fusion.44
  458.4 8.2 fusion.24
  495.0 8.2 pad_maximum_fusion
  509.6 9.5 fusion.61
  523.7 40.2 %all-reduce.4 = (f32[1024]{0:T(1024)S(1)}, f32[1024]{0:T(1024)S(1)}) all-reduce(f32[1024]{0:T(1024)S(1)} %get-tuple-element.62, f32[1024]{0:T(1024)S(1)} %get-tuple-element.60), channel_id=6, replica_groups=mesh['dp'=2,'fsdp'=16] {'dp','fsdp'}, use_global_device_ids=true, to_apply=%region_15.16.clone | all-reduce | flops 2048 | bytes 16384
  575.5 48.9 %reduce-scatter.5.cloned.1.call-done = f32[32,800]{1,0:T(8,128)} async-done(((f32[1024,800]{1,0:T(8,128)}), f32[32,800]{1,0:T(8,128)}) %reduce-scatter.5.cloned.1.call-update) | async-done | bytes 102416 | tf_op jit(solution)/shard_map/reduce_scatter | solution.py:295
  630.1 240.0 %reduce-scatter.9.cloned.1.call-done = f32[32,5632]{1,0:T(8,128)} async-done(((f32[1024,5632]{1,0:T(8,128)}), f32[32,5632]{1,0:T(8,128)}) %reduce-scatter.9.cloned.1.call-update) | async-done | bytes 720912 | tf_op jit(solution)/shard_map/reduce_scatter | solution.py:247
  872.1 144.4 %reduce-scatter.7.cloned.1.call-done = f32[32,1024]{1,0:T(8,128)} async-done(((f32[1024,1024]{1,0:T(8,128)}), f32[32,1024]{1,0:T(8,128)}) %reduce-scatter.7.cloned.1.call-update) | async-done | bytes 131088 | tf_op jit(solution)/shard_map/reduce_scatter | solution.py:296
  1016.5 154.0 %reduce-scatter.11.cloned.1.call-done = f32[88,1024]{1,0:T(8,128)} async-done(((f32[2816,1024]{1,0:T(8,128)}), f32[88,1024]{1,0:T(8,128)}) %reduce-scatter.11.cloned.1.call-update) | async-done | bytes 360464 | tf_op jit(solution)/shard_map/reduce_scatter | solution.py:256
  (208 shorter events, 198.6 us)
Async XLA Ops:
  7.2 62.9 %copy-start.17 = (bf16[512,1024]{1,0:T(8,128)(2,1)S(1)}, bf16[512,1024]{1,0:T(8,128)(2,1)}, u32[]{:S(2)}) copy-start(bf16[512,1024]{1,0:T(8,128)(2,1)} %param.15) | copy-start | bytes 3145732
  7.2 62.9 %all-gather.6.cloned.1.call-start = ((), (), s32[]{:S(2)}) async-start(), calls=%async_computation.4 | async-start | bytes 1892352 | tf_op jit(solution)/shard_map/all_gather | solution.py:178
  8.8 157.1 %all-gather.8.cloned.1.call-start = ((), (), s32[]{:S(2)}) async-start(), calls=%async_computation.5 | async-start | bytes 2162688 | tf_op jit(solution)/shard_map/all_gather | solution.py:179
  9.6 187.9 %all-gather.10.cloned.1.call-start = ((), (), s32[]{:S(2)}) async-start(), calls=%async_computation.6 | async-start | bytes 5947392 | tf_op jit(solution)/shard_map/all_gather | solution.py:210
  10.3 256.1 %all-gather.12.cloned.1.call-start = ((), (), s32[]{:S(2)}) async-start(), calls=%async_computation.7 | async-start | bytes 5947392 | tf_op jit(solution)/shard_map/all_gather | solution.py:211
  10.9 324.6 %all-gather.14.cloned.1.call-start = ((), (), s32[]{:S(2)}) async-start(), calls=%async_computation.8 | async-start | bytes 5947392 | tf_op jit(solution)/shard_map/all_gather | solution.py:212
  11.5 612.9 %reduce-scatter.5.cloned.1.call-start = ((), (), s32[]{:S(2)}) async-start(), calls=%async_computation.9 | async-start | bytes 3784704 | tf_op jit(solution)/shard_map/reduce_scatter | solution.py:295
  56.3 16.5 %copy-start.38 = (f32[1024]{0:T(1024)}, f32[1024]{0:T(1024)S(1)}, u32[]{:S(2)}) copy-start(f32[1024]{0:T(1024)S(1)} %convert_element_type.81) | copy-start | bytes 12292
  58.5 14.2 %copy-start.41 = (f32[512]{0:T(512)}, f32[512]{0:T(512)S(1)}, u32[]{:S(2)}) copy-start(f32[512]{0:T(512)S(1)} %add_rsqrt_fusion.1) | copy-start | bytes 6148
  61.2 17.2 %copy-start.26 = (f32[512,32]{1,0:T(8,128)}, f32[512,32]{1,0:T(8,128)S(1)}, u32[]{:S(2)}) copy-start(f32[512,32]{1,0:T(8,128)S(1)} %get-tuple-element.105) | copy-start | bytes 196612
  170.8 95.7 %copy-start.32 = (bf16[512,1024]{1,0:T(8,128)(2,1)}, bf16[512,1024]{1,0:T(8,128)(2,1)S(1)}, u32[]{:S(2)}) copy-start(bf16[512,1024]{1,0:T(8,128)(2,1)S(1)} %multiply_convert_fusion.4) | copy-start | bytes 3145732
  346.8 7.4 copy-start.46
  346.8 7.4 copy-start.44
  346.9 7.4 copy-start.11
  346.9 7.4 copy-start.43
  385.2 7.5 copy-start.19
  403.5 15.6 %copy-start.16 = (f32[512,16,64]{0,2,1:T(8,128)S(1)}, f32[512,16,64]{0,2,1:T(8,128)}, u32[]{:S(2)}) copy-start(f32[512,16,64]{0,2,1:T(8,128)} %copy.176) | copy-start | bytes 6291460
  428.1 15.8 %copy-start.1 = (bf16[16,512,512]{1,2,0:T(8,128)(2,1)S(1)}, bf16[16,512,512]{1,2,0:T(8,128)(2,1)}, u32[]{:S(2)}) copy-start(bf16[16,512,512]{1,2,0:T(8,128)(2,1)} %copy-done) | copy-start | bytes 25165828
  458.3 8.2 copy-start.31
  458.4 9.0 copy-start.28
  458.4 9.8 copy-start.27
  485.3 384.7 %reduce-scatter.9.cloned.1.call-start = ((), (), s32[]{:S(2)}) async-start(), calls=%async_computation.11 | async-start | bytes 23789568 | tf_op jit(solution)/shard_map/reduce_scatter | solution.py:247
  503.2 513.3 %reduce-scatter.7.cloned.1.call-start = ((), (), s32[]{:S(2)}) async-start(), calls=%async_computation.10 | async-start | bytes 4325376 | tf_op jit(solution)/shard_map/reduce_scatter | solution.py:296
  509.3 661.2 %reduce-scatter.11.cloned.1.call-start = ((), (), s32[]{:S(2)}) async-start(), calls=%async_computation.12 | async-start | bytes 11894784 | tf_op jit(solution)/shard_map/reduce_scatter | solution.py:256
  (33 other events, 109.5 us)
Sparse Core Ops, SparseCore 0:
  11.5 58.5 all-gather.5
  73.0 55.4 all-gather.7
  131.3 66.1 all-gather.9
  200.2 66.2 all-gather.11
  269.2 66.2 all-gather.13
  485.5 138.8 reduce-scatter.4
  626.8 243.2 reduce-scatter.8
  873.0 143.4 reduce-scatter.6
  1019.5 150.9 reduce-scatter.10
where the time goes:
time: 1190 us; the launch traced here: 1180 us
  waiting for transfers between devices  748 us (63%)
  matrix products  202 us (17%)
  blocking collectives  82.3 us (7%)
  local copies, waits for them, and re-layouts  78.7 us (7%)
  other arithmetic  50.5 us (4%)
  between operations  14.9 us (1%)
    reduce_scatter x1, waiting for transfers between devices, local(): lax.psum_scatter(jnp.concatenate([gate_rows, up_rows], axis=1), ('dp', 'f...  240 us
    reduce_scatter x1, waiting for transfers between devices, local(): lax.psum_scatter(down_wgrad, ('dp', 'fsdp'), scatter_dimension=0, tiled=T...  154 us
    reduce_scatter x1, waiting for transfers between devices, local(): lax.psum_scatter(out_wgrad, ('dp', 'fsdp'), scatter_dimension=0, tiled=True)  144 us
    unnamed x2, blocking collectives  82.3 us
    all_gather x1, waiting for transfers between devices, local(): lax.all_gather(w_up, ('dp', 'fsdp'), axis=0, tiled=True)  61.5 us
    all_gather x1, waiting for transfers between devices, local(): lax.all_gather(w_down, ('dp', 'fsdp'), axis=0, tiled=True)  61.4 us
    reduce_scatter x1, waiting for transfers between devices, local(): lax.psum_scatter(factor_wgrad, ('dp', 'fsdp'), scatter_dimension=0, tiled...  48.9 us
    all_gather x1, waiting for transfers between devices, local(): lax.all_gather(w_gate, ('dp', 'fsdp'), axis=0, tiled=True)  26.7 us
  transfers between devices with their start and end apart: 9, of which 8 were waited for; matrix products, arithmetic and copies ran while one was open for 15% of the time, Pallas kernels for 0%

commit v1 on v0

--- a/solution.py
+++ b/solution.py
@@ -3,6 +3,8 @@
 import jax
 import jax.numpy as jnp
 from jax import lax
+from jax.experimental import pallas as pl
+from jax.experimental.pallas import tpu as pltpu
 from jax.sharding import PartitionSpec as P
 
 HEADS = 16
@@ -37,7 +39,8 @@
 
 
 def doc_layout(lengths, length):
-    doc_ends = jnp.cumsum(lengths)
+    order = jnp.arange(lengths.shape[0], dtype=jnp.int32)
+    doc_ends = jnp.sum(jnp.where(order[:, None] >= order[None, :], lengths[None, :], 0), axis=1)
     doc_starts = doc_ends - lengths
     places = jnp.arange(length, dtype=jnp.int32)
     segment = jnp.sum((places[:, None] >= doc_ends[None, :]).astype(jnp.int32), axis=1)
@@ -315,9 +318,711 @@
     )
 
 
+MESH_IDS = pl.DeviceIdType.MESH
+HALF = FF // 2
+OWN_UNITS = 88
+PAD_UNITS = 96
+FACTOR_PAD = 896
+MIB = 2**20
+
+
+def fits_pairs(mesh):
+    return dict(mesh.shape) == {"dp": 2, "fsdp": 16}
+
+
+def place():
+    x = lax.axis_index("dp")
+    f = lax.axis_index("fsdp")
+    return x, lax.div(f, 4), lax.rem(lax.div(f, 2), 2), lax.rem(f, 2)
+
+
+def device(x, z, y, c):
+    return (x, z * 4 + y * 2 + c)
+
+
+def greet(x, z, y, c):
+    partners = [
+        device(x, z, y, 1 - c),
+        device(1 - x, z, y, c),
+        device(x, z, 1 - y, c),
+        device(1 - x, z, y, 1 - c),
+    ]
+    for step in (1, 2, 3):
+        other = lax.rem(z + step, 4)
+        partners += [device(x, other, y, c), device(x, other, y, 1 - c)]
+    barrier = pltpu.get_barrier_semaphore()
+    for partner in partners:
+        pl.semaphore_signal(barrier, inc=1, device_id=partner, device_id_type=MESH_IDS)
+    pl.semaphore_wait(barrier, len(partners))
+
+
+class Wires:
+    def __init__(self, send_sems, recv_sems, local_sems):
+        self.send_sems, self.recv_sems, self.local_sems = send_sems, recv_sems, local_sems
+        self.sent, self.held = 0, 0
+        self.open = []
+
+    def make(self, src, dst, to):
+        at = self.sent
+        self.sent += 1
+        return pltpu.make_async_remote_copy(
+            src_ref=src,
+            dst_ref=dst,
+            send_sem=self.send_sems.at[at],
+            recv_sem=self.recv_sems.at[at],
+            device_id=to,
+            device_id_type=MESH_IDS,
+        )
+
+    def send(self, src, dst, to):
+        copy = self.make(src, dst, to)
+        copy.start()
+        self.open.append(copy)
+        return copy
+
+    def local(self, src, dst):
+        copy = pltpu.make_async_copy(src, dst, self.local_sems.at[self.held])
+        self.held += 1
+        copy.start()
+        return copy
+
+    def drain(self):
+        for copy in self.open:
+            copy.wait_send()
+        self.open = []
+
+
+def arrive(copies):
+    for copy in copies:
+        copy.wait_recv()
+
+
+def gather_kernel(fac, wo, wd, wg, wu, fac_all, out_all, down_all, gate_all, up_all, ss, rs, ls):
+    x, z, y, c = place()
+    x_peer, y_peer, twin = device(1 - x, z, y, c), device(x, z, 1 - y, c), device(x, z, y, 1 - c)
+    z_peers = [lax.rem(z + step, 4) for step in (1, 2, 3)]
+    greet(x, z, y, c)
+    w = Wires(ss, rs, ls)
+    mine = pl.ds(pl.multiple_of(c * HALF, 128), HALF)
+    theirs = pl.ds(pl.multiple_of((1 - c) * HALF, 128), HALF)
+
+    def full_z(src, ref):
+        own = w.local(src, ref.at[x, z, y, c])
+        return own, [w.send(src, ref.at[x, z, y, c], device(x, zz, y, c)) for zz in z_peers]
+
+    def full_two(ref, own, first):
+        own.wait()
+        arrive(first)
+        a = w.send(ref.at[x, :, y, c, 0:16], ref.at[x, :, y, c, 0:16], x_peer)
+        b = w.send(ref.at[x, :, y, c, 16:32], ref.at[x, :, y, c, 16:32], y_peer)
+        return a, b, [w.send(ref.at[x, :, y, c], ref.at[x, :, y, c], twin)]
+
+    def full_three(ref, a, b, down):
+        a.wait_recv()
+        a2 = w.send(ref.at[:, :, y, c, 0:16], ref.at[:, :, y, c, 0:16], y_peer)
+        b.wait_recv()
+        b2 = w.send(ref.at[x, :, :, c, 16:32], ref.at[x, :, :, c, 16:32], x_peer)
+        down.append(w.send(ref.at[1 - x, :, y, c, 0:16], ref.at[1 - x, :, y, c, 0:16], twin))
+        down.append(w.send(ref.at[x, :, 1 - y, c, 16:32], ref.at[x, :, 1 - y, c, 16:32], twin))
+        return a2, b2
+
+    def full_end(ref, a2, b2, down):
+        a2.wait_recv()
+        down.append(w.send(ref.at[:, :, 1 - y, c, 0:16], ref.at[:, :, 1 - y, c, 0:16], twin))
+        b2.wait_recv()
+        down.append(w.send(ref.at[1 - x, :, :, c, 16:32], ref.at[1 - x, :, :, c, 16:32], twin))
+        arrive(down)
+
+    def pair_z(src, ref):
+        own = w.local(src.at[:, mine], ref.at[x, z, y, c])
+        first = []
+        for zz in z_peers:
+            first.append(w.send(src.at[:, mine], ref.at[x, z, y, c], device(x, zz, y, c)))
+            first.append(w.send(src.at[:, theirs], ref.at[x, z, y, c], device(x, zz, y, 1 - c)))
+        first.append(w.send(src.at[:, theirs], ref.at[x, z, y, c], twin))
+        return own, first
+
+    own_f, z_f = full_z(fac, fac_all)
+    own_o, z_o = full_z(wo, out_all)
+    swap = w.make(wd, down_all.at[z, y, 1 - x], device(1 - x, z, y, 1 - c))
+    keep = pltpu.make_async_copy(wd, down_all.at[z, y, x], w.local_sems.at[w.held])
+    w.held += 1
+
+    @pl.when(x == c)
+    def _():
+        keep.start()
+
+    @pl.when(x != c)
+    def _():
+        swap.start()
+
+    a_f, b_f, d_f = full_two(fac_all, own_f, z_f)
+    a_o, b_o, d_o = full_two(out_all, own_o, z_o)
+
+    @pl.when(x == c)
+    def _():
+        keep.wait()
+
+    @pl.when(x != c)
+    def _():
+        swap.wait()
+
+    slot = down_all.at[z, y, x]
+    z_d = [w.send(slot, slot, device(x, zz, y, c)) for zz in z_peers]
+    a2_f, b2_f = full_three(fac_all, a_f, b_f, d_f)
+    own_g, z_g = pair_z(wg, gate_all)
+    a2_o, b2_o = full_three(out_all, a_o, b_o, d_o)
+    own_u, z_u = pair_z(wu, up_all)
+    arrive(z_d)
+    upper, lower = pl.ds(0, PAD_UNITS // 2), pl.ds(PAD_UNITS // 2, PAD_UNITS // 2)
+    view = down_all.at[:, y, x, upper]
+    a_d = w.send(view, view, x_peer)
+    view = down_all.at[:, y, x, lower]
+    b_d = w.send(view, view, y_peer)
+    own_g.wait()
+    arrive(z_g)
+    view = gate_all.at[x, :, y]
+    a_g = w.send(view, view, x_peer)
+    own_u.wait()
+    arrive(z_u)
+    view = up_all.at[x, :, y]
+    b_u = w.send(view, view, y_peer)
+    full_end(fac_all, a2_f, b2_f, d_f)
+    full_end(out_all, a2_o, b2_o, d_o)
+    a_d.wait_recv()
+    view = down_all.at[:, y, :, upper]
+    a2_d = w.send(view, view, y_peer)
+    b_d.wait_recv()
+    view = down_all.at[:, :, x, lower]
+    b2_d = w.send(view, view, x_peer)
+    a_g.wait_recv()
+    view = gate_all.at[:, :, y]
+    a2_g = w.send(view, view, y_peer)
+    b_u.wait_recv()
+    view = up_all.at[x]
+    b2_u = w.send(view, view, x_peer)
+    arrive([a2_d, b2_d, a2_g, b2_u])
+    w.drain()
+
+
+def gather_all(fac, wo, wd, wg, wu):
+    bf16 = jnp.bfloat16
+    shapes = [
+        (2, 4, 2, 2, 32, FACTOR_PAD),
+        (2, 4, 2, 2, 32, 1024),
+        (4, 2, 2, PAD_UNITS, 1024),
+        (2, 4, 2, 2, 32, HALF),
+        (2, 4, 2, 2, 32, HALF),
+    ]
+    anywhere = pl.BlockSpec(memory_space=pl.ANY)
+    return pl.pallas_call(
+        gather_kernel,
+        out_shape=[jax.ShapeDtypeStruct(s, bf16) for s in shapes],
+        in_specs=[anywhere] * 5,
+        out_specs=[anywhere] * 5,
+        scratch_shapes=[
+            pltpu.SemaphoreType.DMA((64,)),
+            pltpu.SemaphoreType.DMA((64,)),
+            pltpu.SemaphoreType.DMA((8,)),
+        ],
+        compiler_params=pltpu.CompilerParams(collective_id=0, has_side_effects=True),
+        name="gather_all",
+    )(fac, wo, wd, wg, wu)
+
+
+BLOCKS = ((0, 512), (512, 512), (1024, 384))
+TILE = 256
+NT = (((1,), (1,)), ((), ()))
+TN = (((0,), (0,)), ((), ()))
+F32, BF16 = jnp.float32, jnp.bfloat16
+
+
+def dot(a, b, dims=None):
+    if dims is None:
+        return jnp.dot(a, b, preferred_element_type=F32)
+    return lax.dot_general(a, b, dims, preferred_element_type=F32)
+
+
+def add_low(dst, src):
+    dst[...] = (dst[...].astype(F32) + src[...].astype(F32)).astype(BF16)
+
+
+def ffn_kernel(
+    n2_in, cot_in, resid, gain, gate_hbm, up_hbm, down_hbm,
+    outputs, resid_grad, gain_part, gate_out, up_out, down_out,
+    n2, cot, n2_t, wg, wu, wd, hid, gg, ug, out_acc, ng_acc, out_twin, ng_twin,
+    g_buf, u_buf, d_buf, d_acc, g1, u1, da1, db1, g2, u2, da2, db2, g3, u3, d3, d_sum,
+    ss, rs, ls,
+):
+    x, z, y, c = place()
+    x_peer, y_peer, twin = device(1 - x, z, y, c), device(x, z, 1 - y, c), device(x, z, y, 1 - c)
+    z_peers = [lax.rem(z + step, 4) for step in (1, 2, 3)]
+    w = Wires(ss, rs, ls)
+    own_n2 = w.local(n2_in, n2.at[0:512])
+    own_cot = w.local(cot_in, cot.at[0:512])
+    loads = []
+    for start, size in BLOCKS:
+        cols = pl.ds(start, size)
+        loads.append(
+            [
+                w.local(gate_hbm.at[:, cols], wg.at[:, cols]),
+                w.local(up_hbm.at[:, cols], wu.at[:, cols]),
+                w.local(down_hbm.at[cols], wd.at[cols]),
+            ]
+        )
+    greet(x, z, y, c)
+    n2_twin = w.send(n2_in, n2.at[512:1024], twin)
+    cot_twin = w.send(cot_in, cot.at[512:1024], twin)
+    own_n2.wait()
+    own_cot.wait()
+
+    def turn(i):
+        rows = pl.ds(pl.multiple_of(i * TILE, TILE), TILE)
+        n2_t[:, rows] = n2[rows, :].T
+
+    def forward(b, low, high):
+        start, size = BLOCKS[b]
+        cols = pl.ds(start, size)
+
+        def tile(i, _):
+            rows = pl.ds(pl.multiple_of(i * TILE, TILE), TILE)
+            n2_rows, cot_rows = n2[rows, :], cot[rows, :]
+            gate = dot(n2_rows, wg[:, cols])
+            up = dot(n2_rows, wu[:, cols])
+            hid_grad = dot(cot_rows, wd[cols, :], NT)
+            sig = jax.nn.sigmoid(gate)
+            silu = gate * sig
+            hidden = (silu * up).astype(BF16)
+            gate_grad = (hid_grad * up * sig * (1.0 + gate * (1.0 - sig))).astype(BF16)
+            up_grad = (hid_grad * silu).astype(BF16)
+            hid[rows, 0:size] = hidden
+            gg[rows, 0:size] = gate_grad
+            ug[rows, 0:size] = up_grad
+            out_part = dot(hidden, wd[cols, :])
+            ng_part = dot(gate_grad, wg[:, cols], NT) + dot(up_grad, wu[:, cols], NT)
+            if b == 0:
+                out_acc[rows, :] = out_part
+                ng_acc[rows, :] = ng_part
+            else:
+                out_acc[rows, :] += out_part
+                ng_acc[rows, :] += ng_part
+            return 0
+
+        lax.fori_loop(low, high, tile, 0)
+
+    def weight_grads(b):
+        start, size = BLOCKS[b]
+        cols = pl.ds(start, size)
+
+        def side(i, _):
+            rows = pl.ds(pl.multiple_of(i * 512, 512), 512)
+            part = dot(n2_t[rows, :], ug[:, 0:size])
+            u_buf[i, :, :, :, cols] = part.astype(BF16).reshape(4, 2, 64, size)
+            part = dot(n2_t[rows, :], gg[:, 0:size])
+            g_buf[i, :, :, :, cols] = part.astype(BF16).reshape(4, 2, 64, size)
+            return 0
+
+        lax.fori_loop(0, 2, side, 0)
+        d_acc[cols, :] = dot(hid[:, 0:size], cot[...], TN)
+
+    def phase_one(b):
+        cols = pl.ds(*BLOCKS[b])
+        u = w.send(u_buf.at[1 - x, :, :, :, cols], u1.at[:, :, :, cols], x_peer)
+        g = w.send(g_buf.at[:, :, 1 - y, :, cols], g1.at[:, :, :, cols], y_peer)
+        return u, g
+
+    def phase_two(b, u, g):
+        cols = pl.ds(*BLOCKS[b])
+        u.wait_recv()
+
+        def add_u(i, _):
+            zz, yy = lax.div(i, 2), lax.rem(i, 2)
+            add_low(u_buf.at[x, zz, yy, :, cols], u1.at[zz, yy, :, cols])
+            return 0
+
+        lax.fori_loop(0, 8, add_u, 0)
+        u = w.send(u_buf.at[x, :, 1 - y, :, cols], u2.at[:, :, cols], y_peer)
+        g.wait_recv()
+
+        def add_g(i, _):
+            xx, zz = lax.div(i, 4), lax.rem(i, 4)
+            add_low(g_buf.at[xx, zz, y, :, cols], g1.at[xx, zz, :, cols])
+            return 0
+
+        lax.fori_loop(0, 8, add_g, 0)
+        g = w.send(g_buf.at[1 - x, :, y, :, cols], g2.at[:, :, cols], x_peer)
+        return u, g
+
+    def phase_three(b, u, g):
+        cols = pl.ds(*BLOCKS[b])
+        last = []
+        for copy, buf, two, three in ((u, u_buf, u2, u3), (g, g_buf, g2, g3)):
+            copy.wait_recv()
+
+            def add(i, _, buf=buf, two=two):
+                add_low(buf.at[x, i, y, :, cols], two.at[i, :, cols])
+                return 0
+
+            lax.fori_loop(0, 4, add, 0)
+            for core, rel in ((c, 0), (1 - c, 1)):
+                rows = pl.ds(pl.multiple_of(core * 32, 32), 32)
+                for step, zz in enumerate(z_peers):
+                    last.append(
+                        w.send(
+                            buf.at[x, zz, y, rows, cols],
+                            three.at[rel, step + 1, :, cols],
+                            device(x, zz, y, core),
+                        )
+                    )
+            rows = pl.ds(pl.multiple_of((1 - c) * 32, 32), 32)
+            last.append(w.send(buf.at[x, z, y, rows, cols], three.at[1, 0, :, cols], twin))
+        return last
+
+    def finish(buf, three, out):
+        rows = pl.ds(pl.multiple_of(c * 32, 32), 32)
+        own = buf[x, z, y, rows, :].astype(F32)
+        for step in (1, 2, 3):
+            own += three[0, step].astype(F32)
+        out[c] = own
+        other = three[1, 0].astype(F32)
+        for step in (1, 2, 3):
+            other += three[1, step].astype(F32)
+        out[1 - c] = other
+
+    for copy in loads[0]:
+        copy.wait()
+    forward(0, 0, 2)
+    turn(0)
+    turn(1)
+    arrive([n2_twin, cot_twin])
+    forward(0, 2, 4)
+    turn(2)
+    turn(3)
+    weight_grads(0)
+    one_0 = phase_one(0)
+    for copy in loads[1]:
+        copy.wait()
+    forward(1, 0, 4)
+    weight_grads(1)
+    one_1 = phase_one(1)
+    two_0 = phase_two(0, *one_0)
+    for copy in loads[2]:
+        copy.wait()
+    forward(2, 2, 4)
+    ng_send = w.send(ng_acc.at[512:1024], ng_twin, twin)
+    out_send = w.send(out_acc.at[512:1024], out_twin, twin)
+    forward(2, 0, 2)
+    weight_grads(2)
+    one_2 = phase_one(2)
+
+    def spread(s, _):
+        rows = d_acc[pl.ds(pl.multiple_of(s * OWN_UNITS, 8), OWN_UNITS), :]
+        rows = jnp.concatenate([rows, jnp.zeros((PAD_UNITS - OWN_UNITS, rows.shape[1]), F32)], axis=0)
+        d_buf[lax.div(s, 4), lax.rem(lax.div(s, 2), 2), lax.rem(s, 2)] = rows.astype(BF16)
+        return 0
+
+    lax.fori_loop(0, 16, spread, 0)
+    upper, lower = pl.ds(0, PAD_UNITS // 2), pl.ds(PAD_UNITS // 2, PAD_UNITS // 2)
+    da = w.send(d_buf.at[:, 1 - y, :, upper], da1, y_peer)
+    db = w.send(d_buf.at[:, :, 1 - x, lower], db1, x_peer)
+    two_1 = phase_two(1, *one_1)
+    arrive([ng_send, out_send])
+
+    def close(i, total):
+        rows = pl.ds(pl.multiple_of(i * 128, 128), 128)
+        base = resid[rows, :]
+        n2[rows, :] = (base + out_acc[rows, :] + out_twin[rows, :]).astype(BF16)
+        grad = ng_acc[rows, :] + ng_twin[rows, :]
+        scale = lax.rsqrt(jnp.mean(base * base, axis=-1, keepdims=True) + EPSILON)
+        unit = base * scale
+        unit_grad = grad * gain[...]
+        back = scale * (unit_grad - unit * jnp.mean(unit_grad * unit, axis=-1, keepdims=True))
+        out_acc[rows, :] = cot[rows, :].astype(F32) + back
+        return total + jnp.sum((grad * unit).reshape(16, 8, 1024), axis=0)
+
+    gain_part[...] = lax.fori_loop(0, 4, close, jnp.zeros((8, 1024), F32))
+    results = [
+        w.local(n2.at[0:512], outputs),
+        w.local(out_acc.at[0:512], resid_grad),
+    ]
+    last = phase_three(0, *two_0)
+    two_2 = phase_two(2, *one_2)
+    last += phase_three(1, *two_1)
+    da.wait_recv()
+    db.wait_recv()
+
+    def add_d(i, _):
+        zz, s = lax.div(i, 2), lax.rem(i, 2)
+        add_low(d_buf.at[zz, y, s, upper], da1.at[zz, s])
+        add_low(d_buf.at[zz, s, x, lower], db1.at[zz, s])
+        return 0
+
+    lax.fori_loop(0, 8, add_d, 0)
+    da = w.send(d_buf.at[:, y, 1 - x, upper], da2, x_peer)
+    db = w.send(d_buf.at[:, 1 - y, x, lower], db2, y_peer)
+    last += phase_three(2, *two_2)
+    da.wait_recv()
+    db.wait_recv()
+
+    def add_d2(i, _):
+        add_low(d_buf.at[i, y, x, upper], da2.at[i])
+        add_low(d_buf.at[i, y, x, lower], db2.at[i])
+        return 0
+
+    lax.fori_loop(0, 4, add_d2, 0)
+    last_d = [
+        w.send(d_buf.at[zz, y, x], d3.at[step], device(x, zz, y, c))
+        for step, zz in enumerate(z_peers)
+    ]
+    arrive(last)
+    finish(u_buf, u3, up_out)
+    finish(g_buf, g3, gate_out)
+    arrive(last_d)
+    d_sum[...] = (
+        d_buf[z, y, x].astype(F32)
+        + d3[0].astype(F32)
+        + d3[1].astype(F32)
+        + d3[2].astype(F32)
+    )
+    swap = w.make(d_sum, down_out, device(1 - x, z, y, 1 - c))
+    keep = pltpu.make_async_copy(d_sum, down_out, w.local_sems.at[w.held])
+    w.held += 1
+
+    @pl.when(x == c)
+    def _():
+        keep.start()
+        keep.wait()
+
+    @pl.when(x != c)
+    def _():
+        swap.start()
+        swap.wait()
+
+    for copy in results:
+        copy.wait()
+    w.drain()
+
+
+def ffn_all(n2, cot, resid, gain, gate_w, up_w, down_w):
+    anywhere, vmem = pl.BlockSpec(memory_space=pl.ANY), pl.BlockSpec(memory_space=pltpu.VMEM)
+    big = lambda *shape: pltpu.VMEM(shape, BF16)
+    wide = lambda *shape: pltpu.VMEM(shape, F32)
+    return pl.pallas_call(
+        ffn_kernel,
+        out_shape=[
+            jax.ShapeDtypeStruct((512, 1024), BF16),
+            jax.ShapeDtypeStruct((512, 1024), F32),
+            jax.ShapeDtypeStruct((8, 1024), F32),
+            jax.ShapeDtypeStruct((2, 32, HALF), F32),
+            jax.ShapeDtypeStruct((2, 32, HALF), F32),
+            jax.ShapeDtypeStruct((PAD_UNITS, 1024), F32),
+        ],
+        in_specs=[anywhere, anywhere, vmem, vmem, anywhere, anywhere, anywhere],
+        out_specs=[anywhere, anywhere, vmem, vmem, vmem, vmem],
+        scratch_shapes=[
+            big(1024, 1024), big(1024, 1024), big(1024, 1024),
+            big(1024, HALF), big(1024, HALF), big(HALF, 1024),
+            big(1024, 512), big(1024, 512), big(1024, 512),
+            wide(1024, 1024), wide(1024, 1024), wide(512, 1024), wide(512, 1024),
+            big(2, 4, 2, 64, HALF), big(2, 4, 2, 64, HALF), big(4, 2, 2, PAD_UNITS, 1024), wide(HALF, 1024),
+            big(2, 4, 64, HALF), big(4, 2, 64, HALF), big(4, 2, PAD_UNITS // 2, 1024), big(4, 2, PAD_UNITS // 2, 1024),
+            big(4, 64, HALF), big(4, 64, HALF), big(4, PAD_UNITS // 2, 1024), big(4, PAD_UNITS // 2, 1024),
+            big(2, 4, 32, HALF), big(2, 4, 32, HALF), big(3, PAD_UNITS, 1024), wide(PAD_UNITS, 1024),
+            pltpu.SemaphoreType.DMA((80,)),
+            pltpu.SemaphoreType.DMA((80,)),
+            pltpu.SemaphoreType.DMA((16,)),
+        ],
+        compiler_params=pltpu.CompilerParams(
+            collective_id=1, has_side_effects=True, vmem_limit_bytes=61 * MIB
+        ),
+        name="ffn_all",
+    )(n2, cot, resid, gain, gate_w, up_w, down_w)
+
+
+def sum_kernel(part, out, own, twin_part, one_a, one_b, two_a, two_b, three, ss, rs, ls):
+    x, z, y, c = place()
+    x_peer, y_peer, twin = device(1 - x, z, y, c), device(x, z, 1 - y, c), device(x, z, y, 1 - c)
+    z_peers = [lax.rem(z + step, 4) for step in (1, 2, 3)]
+    w = Wires(ss, rs, ls)
+    load = w.local(part.at[:, :, :, c], own)
+    greet(x, z, y, c)
+    first = w.send(part.at[:, :, :, 1 - c], twin_part, twin)
+    load.wait()
+    first.wait_recv()
+
+    def add(i, _):
+        xx, zz, yy = lax.div(i, 8), lax.rem(lax.div(i, 2), 4), lax.rem(i, 2)
+        add_low(own.at[xx, zz, yy], twin_part.at[xx, zz, yy])
+        return 0
+
+    lax.fori_loop(0, 16, add, 0)
+    upper, lower = pl.ds(0, 16), pl.ds(16, 16)
+    a = w.send(own.at[:, :, 1 - y, upper], one_a, y_peer)
+    b = w.send(own.at[1 - x, :, :, lower], one_b, x_peer)
+    a.wait_recv()
+    b.wait_recv()
+
+    def add_one(i, _):
+        s, zz = lax.div(i, 4), lax.rem(i, 4)
+        add_low(own.at[s, zz, y, upper], one_a.at[s, zz])
+        add_low(own.at[x, zz, s, lower], one_b.at[zz, s])
+        return 0
+
+    lax.fori_loop(0, 8, add_one, 0)
+    a = w.send(own.at[1 - x, :, y, upper], two_a, x_peer)
+    b = w.send(own.at[x, :, 1 - y, lower], two_b, y_peer)
+    a.wait_recv()
+    b.wait_recv()
+
+    def add_two(i, _):
+        add_low(own.at[x, i, y, upper], two_a.at[i])
+        add_low(own.at[x, i, y, lower], two_b.at[i])
+        return 0
+
+    lax.fori_loop(0, 4, add_two, 0)
+    last = [
+        w.send(own.at[x, zz, y], three.at[step], device(x, zz, y, c))
+        for step, zz in enumerate(z_peers)
+    ]
+    arrive(last)
+    out[...] = (
+        own[x, z, y].astype(F32)
+        + three[0].astype(F32)
+        + three[1].astype(F32)
+        + three[2].astype(F32)
+    )
+    w.drain()
+
+
+def sum_all(part):
+    width = part.shape[-1]
+    big = lambda *shape: pltpu.VMEM(shape, BF16)
+    return pl.pallas_call(
+        sum_kernel,
+        out_shape=jax.ShapeDtypeStruct((32, width), F32),
+        in_specs=[pl.BlockSpec(memory_space=pl.ANY)],
+        out_specs=pl.BlockSpec(memory_space=pltpu.VMEM),
+        scratch_shapes=[
+            big(2, 4, 2, 32, width), big(2, 4, 2, 32, width),
+            big(2, 4, 16, width), big(4, 2, 16, width), big(4, 16, width), big(4, 16, width),
+            big(3, 32, width),
+            pltpu.SemaphoreType.DMA((16,)),
+            pltpu.SemaphoreType.DMA((16,)),
+            pltpu.SemaphoreType.DMA((2,)),
+        ],
+        compiler_params=pltpu.CompilerParams(
+            collective_id=2, has_side_effects=True, vmem_limit_bytes=40 * MIB
+        ),
+        name="sum_all",
+    )(part)
+
+
+def local_paired(
+    inputs, doc_lengths, w_aq, w_bq, w_ak, w_bk, w_av, w_bv,
+    w_out, w_gate, w_up, w_down, gain_attn, gain_ffn, cotangent,
+):
+    length = inputs.shape[0]
+    spare = jnp.zeros((32, FACTOR_PAD - 802), BF16)
+    fac = jnp.concatenate(
+        [w_aq, w_bq, w_ak, w_bk, w_av, w_bv, gain_attn[:, None], gain_ffn[:, None], spare], axis=1
+    )
+    wd = jnp.pad(w_down, ((0, PAD_UNITS - OWN_UNITS), (0, 0)))
+    fac_all, out_all, down_all, gate_all, up_all = gather_all(fac, w_out, wd, w_gate, w_up)
+    fac_all = fac_all.reshape(1024, FACTOR_PAD)
+    factor_w = fac_all[:, :800]
+    gain_one, gain_two = fac_all[:, 800].astype(F32), fac_all[:, 801].astype(F32)
+    out_w = out_all.reshape(1024, 1024)
+    gate_w = gate_all.reshape(1024, HALF)
+    up_w = up_all.reshape(1024, HALF)
+    down_w = down_all.reshape(16, PAD_UNITS, 1024)[:, :OWN_UNITS].reshape(HALF, 1024)
+
+    segment, places = doc_layout(doc_lengths[0], length)
+    cos_table, sin_table = rotation(places)
+    start_vals = inputs.astype(jnp.float32)
+    normed_one, unit_one, scale_one = normalize(start_vals, gain_one)
+    normed_low = normed_one.astype(jnp.bfloat16)
+    factors = jnp.dot(normed_low, factor_w, preferred_element_type=jnp.float32)
+    pieces = split_columns(factors)
+    a_q = pieces[0].reshape(length, RANK_Q, HEADS)
+    b_q = pieces[1].reshape(length, RANK_Q, HEAD_DIM)
+    a_k = pieces[2].reshape(length, RANK_KV, HEADS)
+    b_k = pieces[3].reshape(length, RANK_KV, HEAD_DIM)
+    a_v = pieces[4].reshape(length, RANK_KV, HEADS)
+    b_v = pieces[5].reshape(length, RANK_KV, HEAD_DIM)
+    bq_rot = rotate(b_q, cos_table, sin_table)
+    bk_rot = rotate(b_k, cos_table, sin_table)
+    queries = (jnp.einsum("trh,trd->thd", a_q, bq_rot, precision=PRECISE) / RANK_Q).astype(BF16)
+    keys_low = (jnp.einsum("trh,trd->thd", a_k, bk_rot, precision=PRECISE) / RANK_KV).astype(BF16)
+    values = (jnp.einsum("trh,trd->thd", a_v, b_v, precision=PRECISE) / RANK_KV).astype(BF16)
+    attended, log_totals = attend_forward(queries, keys_low, values, segment)
+    mixed = attended.astype(jnp.bfloat16).reshape(length, HEADS * HEAD_DIM)
+    resid = start_vals + jnp.dot(mixed, out_w, preferred_element_type=jnp.float32)
+    normed_two, _, _ = normalize(resid, gain_two)
+
+    outputs, resid_grad, gain_two_part, gate_shard, up_shard, down_shard = ffn_all(
+        normed_two.astype(BF16), cotangent, resid, gain_two[None, :], gate_w, up_w, down_w
+    )
+    gate_shard = jnp.concatenate([gate_shard[0], gate_shard[1]], axis=1)
+    up_shard = jnp.concatenate([up_shard[0], up_shard[1]], axis=1)
+    down_shard = down_shard[:OWN_UNITS]
+    gain_two_grad = jnp.sum(gain_two_part, axis=0)
+
+    branch_grad = resid_grad.astype(jnp.bfloat16)
+    out_wgrad = jnp.einsum("tc,td->cd", mixed, branch_grad, preferred_element_type=jnp.float32)
+    mixed_grad = jnp.einsum("td,cd->tc", branch_grad, out_w, preferred_element_type=jnp.float32)
+    mixed_grad = mixed_grad.astype(jnp.bfloat16).reshape(length, HEADS, HEAD_DIM)
+    query_grad, key_grad, value_grad = attend_backward(
+        queries, keys_low, values, segment, log_totals, mixed_grad
+    )
+    a_q_grad, bq_rot_grad = factor_back(query_grad, a_q, bq_rot, RANK_Q)
+    a_k_grad, bk_rot_grad = factor_back(key_grad, a_k, bk_rot, RANK_KV)
+    a_v_grad, b_v_grad = factor_back(value_grad, a_v, b_v, RANK_KV)
+    neg_sin = -sin_table
+    b_q_grad = rotate(bq_rot_grad, cos_table, neg_sin)
+    b_k_grad = rotate(bk_rot_grad, cos_table, neg_sin)
+    factor_grad = jnp.concatenate(
+        [
+            part.reshape(length, -1)
+            for part in (a_q_grad, b_q_grad, a_k_grad, b_k_grad, a_v_grad, b_v_grad)
+        ],
+        axis=1,
+    ).astype(jnp.bfloat16)
+    factor_wgrad = jnp.einsum(
+        "td,tc->dc", normed_low, factor_grad, preferred_element_type=jnp.float32
+    )
+    normed_one_grad = jnp.einsum(
+        "tc,dc->td", factor_grad, factor_w, preferred_element_type=jnp.float32
+    )
+    input_norm_grad, gain_one_grad = norm_back(normed_one_grad, unit_one, scale_one, gain_one)
+    input_grad = resid_grad + input_norm_grad
+    part = jnp.concatenate(
+        [
+            factor_wgrad,
+            gain_one_grad[:, None],
+            gain_two_grad[:, None],
+            jnp.zeros((1024, FACTOR_PAD - 802), F32),
+            out_wgrad,
+        ],
+        axis=1,
+    ).astype(BF16)
+    shard = sum_all(part.reshape(2, 4, 2, 2, 32, FACTOR_PAD + 1024))
+    shard_pieces = split_columns(shard)
+    return (
+        outputs,
+        input_grad,
+        *shard_pieces,
+        shard[:, FACTOR_PAD:],
+        gate_shard,
+        up_shard,
+        down_shard,
+        shard[:, 800],
+        shard[:, 801],
+    )
+
+
 def solution(mesh):
     return jax.shard_map(
-        local,
+        local_paired if fits_pairs(mesh) else local,
         mesh=mesh,
         in_specs=(
             P(("dp", "fsdp"), None),

time: 1190 us -> 569 us (0.48)
  waiting for transfers between devices: 748 us -> 0 us
  Pallas kernels: 0 us -> 295 us
  blocking collectives: 82.3 us -> 0 us
  matrix products: 202 us -> 144 us
  between operations: 14.9 us -> 1.5 us
    reduce_scatter x4 -> x0, waiting for transfers between devices: 587 us -> none  [the longest x1 240 us: local(): lax.psum_scatter(jnp.concatenate([gate_rows, up_rows], axis=1), ('dp', 'f...]
    pallas_call x0 -> x3, Pallas kernels: none -> 295 us  [the longest x1 129 us: gather_all(): pl.pallas_call(gather_kernel, out_shape=[jax.ShapeDtypeStruct(s, bf16) fo...]
    all_gather x5 -> x0, waiting for transfers between devices: 159 us -> none  [the longest x1 61.5 us: local(): lax.all_gather(w_up, ('dp', 'fsdp'), axis=0, tiled=True)]
    unnamed x2 -> x0, blocking collectives: 82.3 us -> none
    dot_general x18 -> x9, matrix products: 110 us -> 46 us  [the longest x1 10.8 us: local_paired(): jnp.einsum('trh,trd->thd', a_q, bq_rot, precision=PRECISE) / RANK_Q]
    unnamed x111 -> x88, local copies, waits for them, and re-layouts: 24.2 us -> 15.2 us
  transfers between devices with their start and end apart: 9 -> 0, of which waited for: 8 -> 0; matrix products, arithmetic and copies ran while one was open for 15% -> 0% of each run, Pallas kernels for 0% -> 0%
where the time goes in v1:
time: 569 us; the launch traced here: 565 us
  Pallas kernels  295 us (52%)
  matrix products  144 us (25%)
  local copies, waits for them, and re-layouts  84.1 us (15%)
  other arithmetic  40.5 us (7%)
    pallas_call x1, Pallas kernels, gather_all(): pl.pallas_call(gather_kernel, out_shape=[jax.ShapeDtypeStruct(s, bf16) fo...  129 us
    pallas_call x1, Pallas kernels, ffn_all(): pl.pallas_call(ffn_kernel, out_shape=[jax.ShapeDtypeStruct((512, 1024), B...  119 us
    pallas_call x1, Pallas kernels, sum_all(): pl.pallas_call(sum_kernel, out_shape=jax.ShapeDtypeStruct((32, width), F3...  47 us
    dot_general x3, matrix products, factor_back(): jnp.einsum('thd,trd->trh', full_grad, b_part, precision=PRECISE)  30.1 us
    dot_general x3, matrix products, factor_back(): jnp.einsum('thd,trh->trd', full_grad, a_part, precision=PRECISE)  17.3 us
    unnamed x88, local copies, waits for them, and re-layouts  15.2 us
    dot_general x1, matrix products, one_block(): jnp.einsum('thd,shd->hts', mixed_grad, values, preferred_element_type=jnp...  11.9 us
    convert_element_type x1, other arithmetic, one_block(): score_grad = (attn_probs * (probs_grad - inner_sum)).astype(jnp.bfloat16)  11.8 us

profile of v1, /device:TPU:0, one launch (start us, length us, event | category | flops | bytes accessed | tf_op | source)
XLA Modules:
  0.0 565.1 jit_solution(8530554408238768003)
XLA Ops:
  5.4 129.3 %gather_all.1 = (bf16[2,4,2,2,32,896]{5,4,3,2,1,0:T(8,128)(2,1)}, bf16[2,4,2,2,32,1024]{5,4,3,2,1,0:T(8,128)(2,1)}, bf16[4,2,2,96,1024]{4,3,2,1,0:T(8,128)(2,1)}...) custom-call(bf16[32,896]{1,0:T(8,128)(2,1)} %concatenate.38.fac, bf16[32,1024]{1,0:T(8,128)(2,1)} %wo.1, ...), custom_call_target="tpu_custom_call" | custom-call | tf_op jit(solution)/shard_map/gather_all/pallas_call | solution.py:518
  146.0 8.9 %fusion.46 = f32[512,16,64]{2,1,0:T(8,128)} fusion(f32[512,2,16]{2,1,0:T(2,128)S(1)} %copy.206, f32[512,2,32]{2,1,0:T(2,128)S(1)} %get-tuple-element.108, f32[512,2,32]{2,1,0:T(2,128)S(1)} %get-tuple-element.107), kind=kOutput, calls=%fused_computation.110 | convolution fusion | flops 12648448 | bytes 2424832 | tf_op jit(solution)/shard_map/trh,trd->thd/dot_general | solution.py:955
  162.9 4.7 multiply_subtract_fusion
  169.6 10.8 %fusion.29 = f32[512,16,64]{2,1,0:T(8,128)} fusion(f32[512,6,16]{2,1,0:T(8,128)} %copy.202, f32[512,6,32]{2,1,0:T(8,128)} %get-tuple-element.98, f32[512,6,32]{2,1,0:T(8,128)} %get-tuple-element.97), kind=kOutput, calls=%fused_computation.54 | convolution fusion | flops 37945344 | bytes 3080192 | tf_op jit(solution)/shard_map/trh,trd->thd/dot_general | solution.py:954
  184.6 8.9 %fusion.53 = (f32[16,512]{1,0:T(8,128)S(1)}, f32[16,512,512]{1,2,0:T(8,128)}) fusion(f32[512,16,64]{0,2,1:T(8,128)S(1)} %copy.207, f32[512,16,64]{0,2,1:T(8,128)} %copy.203, pred[512,512]{0,1:T(8,128)(4,1)S(1)} %fusion.27), kind=kOutput, calls=%fused_computation.117 | convolution fusion | flops 551542784 | bytes 21266432 | tf_op jit(solution)/shard_map/while/body/eval_jaxpr/thd,shd->hts/dot_general | solution.py:91
  193.5 8.3 %fusion = f32[16,512]{1,0:T(8,128)S(1)} fusion(f32[16,512,512]{1,2,0:T(8,128)} %get-tuple-element.127, f32[16,512]{1,0:T(8,128)S(1)} %get-tuple-element.126), kind=kLoop, calls=%fused_computation.6 | loop fusion | flops 8380416 | bytes 16842752 | tf_op jit(solution)/shard_map/while/body/eval_jaxpr/reduce_sum | solution.py:107
  203.1 9.2 %fusion.54 = f32[512,16,64]{2,1,0:T(8,128)} fusion(f32[512,2,16]{2,1,0:T(2,128)} %copy.197, f32[512,2,64]{2,1,0:T(2,128)S(1)} %copy.198), kind=kOutput, calls=%fused_computation.118 | convolution fusion | flops 12582912 | bytes 2424832 | tf_op jit(solution)/shard_map/trh,trd->thd/dot_general | solution.py:956
  216.5 9.4 %fusion.24 = bf16[16,64,512]{2,1,0:T(8,128)(2,1)S(1)} fusion(f32[16,512,512]{1,2,0:T(8,128)} %get-tuple-element.127, f32[16,512]{1,0:T(8,128)S(1)} %fusion, f32[16,512]{1,0:T(8,128)S(1)} %get-tuple-element.126, f32[512,16,64]{0,2,1:T(8,128)} %copy.199), kind=kOutput, calls=%fused_computation.45 | convolution fusion | flops 551026688 | bytes 19988480 | tf_op jit(solution)/shard_map/while/body/eval_jaxpr/hts,shd->thd/dot_general | solution.py:109
  234.7 118.9 %ffn_all.1 = (bf16[512,1024]{1,0:T(8,128)(2,1)}, f32[512,1024]{1,0:T(8,128)}, f32[8,1024]{1,0:T(8,128)}, f32[2,32,1408]{2,1,0:T(8,128)}, f32[2,32,1408]{2,1,0:T(8,128)}, /*index=5*/f32[96,1024]{1,0:T(8,128)}) custom-call(bf16[512,1024]{1,0:T(8,128)(2,1)} %multiply_convert_fusion.1.n2_in, bf16[512,1024]{1,0:T(8,128)(2,1)} %cot_in.1, ...), custom_call_target="tpu_custom_call" | custom-call | tf_op jit(solution)/shard_map/ffn_all/pallas_call | solution.py:810
  365.5 10.1 %fusion.17 = f32[512,16,64]{0,2,1:T(8,128)} fusion(bf16[512,16,64]{0,2,1:T(8,128)(2,1)} %bitcast.83, f32[16,512,512]{1,2,0:T(8,128)} %get-tuple-element.127, f32[16,512]{1,0:T(8,128)S(1)} %log_add_fusion), kind=kOutput, calls=%fused_computation.39 | convolution fusion | flops 545259520 | bytes 19955712 | tf_op jit(solution)/shard_map/while/body/eval_jaxpr/hts,thd->shd/dot_general | solution.py:129
  375.6 4.8 copy.226
  380.4 6.0 %fusion.25 = bf16[512,2,64]{2,1,0:T(2,128)(2,1)S(1)} fusion(f32[512,2,16]{2,1,0:T(2,128)} %copy.197, f32[512,16,64]{2,1,0:T(8,128)} %copy.226), kind=kOutput, calls=%fused_computation.49 | convolution fusion | flops 12713984 | bytes 2293760 | tf_op jit(solution)/shard_map/thd,trh->trd/dot_general | solution.py:157
  386.6 9.1 %fusion.55 = f32[512,2,16]{2,1,0:T(2,128)} fusion(f32[512,2,64]{2,1,0:T(2,128)S(1)} %copy.198, f32[512,16,64]{2,1,0:T(8,128)} %copy.226), kind=kOutput, calls=%fused_computation.119 | convolution fusion | flops 12582912 | bytes 2424832 | tf_op jit(solution)/shard_map/thd,trd->trh/dot_general | solution.py:156
  396.9 11.9 %multiply_reduce_fusion = (f32[16,512]{1,0:T(8,128)S(1)}, f32[16,512,512]{1,2,0:T(8,128)}) fusion(f32[16,512,512]{1,2,0:T(8,128)} %get-tuple-element.127, f32[16,512]{1,0:T(8,128)S(1)} %log_add_fusion, bf16[512,16,64]{0,2,1:T(8,128)(2,1)} %bitcast.84, f32[512,16,64]{0,2,1:T(8,128)} %copy.199), kind=kOutput, calls=%fused_computation.1 | convolution fusion | flops 550494208 | bytes 36765696 | tf_op jit(solution)/shard_map/while/body/eval_jaxpr/thd,shd->hts/dot_general | solution.py:132
  408.8 11.8 %multiply_convert_fusion = bf16[16,512,512]{1,2,0:T(8,128)(2,1)S(1)} fusion(f32[16,512,512]{1,2,0:T(8,128)} %get-tuple-element.131, f32[16,512,512]{1,2,0:T(8,128)} %get-tuple-element.127, f32[16,512]{1,0:T(8,128)S(1)} %get-tuple-element.130, f32[16,512]{1,0:T(8,128)S(1)} %log_add_fusion), kind=kLoop, calls=%fused_computation | loop fusion | flops 16777216 | bytes 42008576 | tf_op jit(solution)/shard_map/while/body/eval_jaxpr/convert_element_type | solution.py:136
  427.9 4.9 copy.219
  432.8 5.6 convolution_multiply_fusion.2
  440.8 10.0 %fusion.45 = f32[512,2,16]{2,1,0:T(2,128)} fusion(f32[512,16,64]{2,1,0:T(8,128)} %copy.219, f32[512,2,32]{2,1,0:T(2,128)} %copy-done.12, f32[512,2,32]{2,1,0:T(2,128)S(1)} %copy-done.11), kind=kOutput, calls=%fused_computation.109 | convolution fusion | flops 12648448 | bytes 2424832 | tf_op jit(solution)/shard_map/thd,trd->trh/dot_general | solution.py:156
  452.1 6.1 %multiply_bitcast_fusion.1 = f32[512,16,64]{0,2,1:T(8,128)} fusion(bf16[16,512,512]{1,2,0:T(8,128)(2,1)} %copy-done.1, f32[512,16,64]{0,2,1:T(8,128)S(1)} %copy.207), kind=kOutput, calls=%fused_computation.29 | convolution fusion | flops 538443776 | bytes 12582912 | tf_op jit(solution)/shard_map/while/body/eval_jaxpr/hts,shd->thd/dot_general | solution.py:138
  458.2 5.0 copy.212
  463.1 5.7 %convolution_multiply_fusion = f32[512,6,64]{2,1,0:T(8,128)S(1)} fusion(f32[512,6,16]{2,1,0:T(8,128)S(1)} %copy-done.3, f32[512,16,64]{2,1,0:T(8,128)} %copy.212), kind=kOutput, calls=%fused_computation.40 | convolution fusion | flops 37945344 | bytes 3080192 | tf_op jit(solution)/shard_map/thd,trh->trd/dot_general | solution.py:157
  474.7 11.0 %fusion.28 = f32[512,6,16]{2,1,0:T(8,128)} fusion(f32[512,16,64]{2,1,0:T(8,128)} %copy.212, f32[512,6,32]{2,1,0:T(8,128)} %get-tuple-element.98, f32[512,6,32]{2,1,0:T(8,128)S(1)} %copy-done.2), kind=kOutput, calls=%fused_computation.53 | convolution fusion | flops 37945344 | bytes 3080192 | tf_op jit(solution)/shard_map/thd,trd->trh/dot_general | solution.py:156
  500.8 7.3 %concatenate.47.part = bf16[2,4,2,2,32,1920]{5,4,3,2,1,0:T(8,128)(2,1)} concatenate(bf16[2,4,2,2,32,800]{5,4,3,2,1,0:T(8,128)(2,1)S(1)} %bitcast.85, bf16[2,4,2,2,32,1]{5,4,3,2,1,0:T(8,128)(2,1)S(1)} %concatenate.50, bf16[2,4,2,2,32,1]{5,4,3,2,1,0:T(8,128)(2,1)S(1)} %concatenate.51, bf16[2,4,2,2,32,94]{5,4,3,2,1,0:T(8,128)(2,1)} %broadcast_in_dim.137, ...), dimensions={5} | concatenate | bytes 7864320 | tf_op jit(solution)/shard_map/concatenate | solution.py:998
  510.2 47.0 %sum_all.1 = f32[32,1920]{1,0:T(8,128)S(1)} custom-call(bf16[2,4,2,2,32,1920]{5,4,3,2,1,0:T(8,128)(2,1)S(1)} %copy-done), custom_call_target="tpu_custom_call" | custom-call | tf_op jit(solution)/shard_map/sum_all/pallas_call | solution.py:900
  (164 shorter events, 98.7 us)
Async XLA Ops:
  0.6 136.4 %copy-start.5 = (bf16[512,1024]{1,0:T(8,128)(2,1)S(1)}, bf16[512,1024]{1,0:T(8,128)(2,1)}, u32[]{:S(2)}) copy-start(bf16[512,1024]{1,0:T(8,128)(2,1)} %param.15) | copy-start | bytes 3145732
  162.9 4.8 slice-start.1
  180.4 4.0 copy-start.30
  193.5 8.3 %copy-start.23 = (f32[512,128]{0,1:T(8,128)S(1)}, f32[512,128]{0,1:T(8,128)}, u32[]{:S(2)}) copy-start(f32[512,128]{0,1:T(8,128)} %get-tuple-element.103) | copy-start | bytes 786436
  216.5 9.4 %copy-start.6 = (bf16[512,1024]{1,0:T(8,128)(2,1)S(1)}, bf16[512,1024]{1,0:T(8,128)(2,1)}, u32[]{:S(2)}) copy-start(bf16[512,1024]{1,0:T(8,128)(2,1)} %param.15) | copy-start | bytes 3145732
  216.5 9.4 %copy-start.17 = (bf16[2,4,2,2,32,1024]{5,4,3,2,1,0:T(8,128)(2,1)S(1)}, bf16[2,4,2,2,32,1024]{5,4,3,2,1,0:T(8,128)(2,1)}, u32[]{:S(2)}) copy-start(bf16[2,4,2,2,32,1024]{5,4,3,2,1,0:T(8,128)(2,1)} %get-tuple-element.83) | copy-start | bytes 6291460
  225.9 2.7 copy-start.24
  229.8 4.9 copy-start.28
  229.8 3.0 copy-start.14
  353.6 2.9 copy-start.19
  356.5 4.0 copy-start.18
  408.8 15.1 %copy-start.4 = (f32[512,16,64]{0,2,1:T(8,128)S(1)}, f32[512,16,64]{0,2,1:T(8,128)}, u32[]{:S(2)}) copy-start(f32[512,16,64]{0,2,1:T(8,128)} %copy.203) | copy-start | bytes 6291460
  420.7 3.3 copy-start.1
  427.9 4.9 copy-start.9
  432.8 5.6 copy-start.15
  458.2 5.0 copy-start.3
  463.1 5.7 %copy-start.16 = (f32[512,32]{1,0:T(8,128)S(1)}, f32[512,32]{1,0:T(8,128)}, u32[]{:S(2)}) copy-start(f32[512,32]{1,0:T(8,128)} %get-tuple-element.123) | copy-start | bytes 196612
  471.0 3.7 copy-start.2
  485.8 3.2 copy-start.7
  485.8 3.2 copy-start.33
  485.8 3.2 copy-start.36
  494.5 5.1 copy-start.31
  510.2 51.0 %copy-start.20 = (f32[512,1024]{1,0:T(8,128)S(1)}, f32[512,1024]{1,0:T(8,128)}, u32[]{:S(2)}) copy-start(f32[512,1024]{1,0:T(8,128)} %get-tuple-element.88) | copy-start | bytes 6291460
  510.2 51.0 %copy-start.21 = (f32[512,1024]{1,0:T(8,128)S(1)}, f32[512,1024]{1,0:T(8,128)}, u32[]{:S(2)}) copy-start(f32[512,1024]{1,0:T(8,128)} %get-tuple-element.132) | copy-start | bytes 6291460
  (16 other events, 26.5 us)
